TPU v7x, 32 devices: a whole 2x2x4 slice. The times are simulated.
32 devices in a mesh: seq: 16 (over z, y, x), exp: 2 (over core).
Axes of the slice: x: 2, y: 2, z: 4, core: 2. Of those that a mesh axis runs over, the one named last changes fastest.
Arguments:
- queries: bfloat16 [2048, 7168], P('seq', 'exp'), may hold values from -8 to 8
- keys: bfloat16 [2048, 7168], P('seq', 'exp'), may hold values from -8 to 8
- values: bfloat16 [2048, 7168], P('seq', 'exp'), may hold values from -34 to 34
- branch_gates: float32 [2048, 2, 56], P('seq', None, 'exp'), may hold values from 0.1 to 1
- block_choice: int32 [32, 8], P('seq'), may hold values from 0 to 14, as said below
- norm_gain: float32 [7168], P('exp'), may hold values from 0.5 to 1.5
- expert_ids: int32 [2048, 8], P('seq'), may hold values from 0 to 15, all different within a row; in each aligned block of 128 rows (0 to 127, 128 to 255, ...) at most 80 rows name the same one
- route_scores: float32 [2048, 8], P('seq'), may hold values from 0.05 to 1
- w_gate_up: bfloat16 [16, 7168, 2, 1536], P('seq', 'exp'), may hold values from -0.0625 to 0.0625
- w_down: bfloat16 [16, 1536, 7168], P('seq', None, 'exp'), may hold values from -0.15625 to 0.15625
Outputs:
- mixed: bfloat16 [2048, 7168], P('seq', 'exp')
Inputs may be any that keep to these rules, and one draw needn't show every extreme that they name: `block_choice`: each row holds offset 0 and 7 other distinct offsets. `expert_ids`: each row names 8 different experts; within each aligned block of 128 rows (the rows of one index of seq) no expert is named more than 80 times, and that many is reached.
All inputs are finite; a program needn't handle non-finite values.
Results may differ from a plain program's by a relative error of at most 0.029.
Values may be sent and summed in bfloat16 or wider, within the bound.
A program may use at most 128 MiB of HBM per device.

v0:
```python
import jax
import jax.numpy as jnp
from jax import lax
from jax.sharding import PartitionSpec as P

HD = 128
D = 7168
BLOCK = 64
WINDOW = 15


EPSILON = 1e-06
ROUTE_SCALE = 2.5
MASKED_SCORE = -1e30


def passed_along(shard, axis, by):
    peers = lax.axis_size(axis)
    pairs = [(i, i + by) for i in range(peers) if 0 <= i + by < peers]
    return lax.ppermute(shard, axis, pairs)


def local(
    queries,
    keys,
    values,
    branch_gates,
    block_choice,
    norm_gain,
    expert_ids,
    route_scores,
    w_gate_up,
    w_down,
):
    tokens_here = queries.shape[0]
    features = queries.shape[1]
    heads_here = features // HD
    blocks_here = tokens_here // BLOCK
    device_row = lax.axis_index("seq")
    seq_devices = lax.axis_size("seq")
    score_scale = HD ** (-0.5)
    query_heads = queries.reshape(tokens_here, heads_here, HD)
    positions = jnp.arange(tokens_here, dtype=jnp.int32)
    query_block = device_row * blocks_here + positions // BLOCK
    query_pos = device_row * tokens_here + positions
    chosen = jnp.repeat(block_choice, BLOCK, axis=0)
    local_kv = jnp.stack([keys, values])
    pooled = jnp.mean(
        local_kv.astype(jnp.float32).reshape(2, blocks_here, BLOCK, features), axis=2
    ).astype(jnp.bfloat16)
    everyone = lax.all_gather(pooled, "seq", axis=1, tiled=True)
    all_blocks = everyone.shape[1]
    pooled_keys = everyone[0].reshape(all_blocks, heads_here, HD)
    pooled_values = everyone[1].reshape(all_blocks, heads_here, HD)
    scores = (
        jnp.einsum("qhd,chd->hqc", query_heads, pooled_keys, preferred_element_type=jnp.float32)
        * score_scale
    )
    earlier = jnp.arange(all_blocks, dtype=jnp.int32)[None, :] < query_block[:, None]
    masked = jnp.where(earlier[None], scores, MASKED_SCORE)
    row_max = jnp.max(masked, axis=2, keepdims=True)
    row_max = jnp.where(row_max > 0.5 * MASKED_SCORE, row_max, 0.0)
    weights = jnp.where(earlier[None], jnp.exp(scores - row_max), 0.0)
    weight_sum = jnp.sum(weights, axis=2)
    coarse_out = jnp.einsum(
        "hqc,chd->hqd",
        weights.astype(jnp.bfloat16),
        pooled_values,
        preferred_element_type=jnp.float32,
    )
    coarse_out = coarse_out / jnp.maximum(weight_sum, 1.0)[..., None]

    def attend(carried, kv_piece, first_block):
        running_max, denominator, numerator = carried
        key_count = kv_piece.shape[1]
        key_heads = kv_piece[0].reshape(key_count, heads_here, HD)
        value_heads = kv_piece[1].reshape(key_count, heads_here, HD)
        key_offsets = jnp.arange(key_count, dtype=jnp.int32)
        key_block = first_block + key_offsets // BLOCK
        key_pos = first_block * BLOCK + key_offsets
        block_gap = query_block[:, None] - key_block[None, :]
        picked = jnp.any(chosen[:, :, None] == block_gap[:, None, :], axis=1)
        allowed = picked & (key_block >= 0)[None, :] & (key_pos[None, :] <= query_pos[:, None])
        piece_scores = (
            jnp.einsum("qhd,khd->hqk", query_heads, key_heads, preferred_element_type=jnp.float32)
            * score_scale
        )
        piece_masked = jnp.where(allowed[None], piece_scores, MASKED_SCORE)
        updated_max = jnp.maximum(running_max, jnp.max(piece_masked, axis=2))
        piece_weights = jnp.where(
            allowed[None], jnp.exp(piece_scores - updated_max[..., None]), 0.0
        )
        rescale = jnp.exp(running_max - updated_max)
        denominator = denominator * rescale + jnp.sum(piece_weights, axis=2)
        numerator = numerator * rescale[..., None] + jnp.einsum(
            "hqk,khd->hqd",
            piece_weights.astype(jnp.bfloat16),
            value_heads,
            preferred_element_type=jnp.float32,
        )
        return (updated_max, denominator, numerator)

    carried = (
        jnp.full((heads_here, tokens_here), MASKED_SCORE, jnp.float32),
        jnp.zeros((heads_here, tokens_here), jnp.float32),
        jnp.zeros((heads_here, tokens_here, HD), jnp.float32),
    )
    carried = attend(carried, local_kv, device_row * blocks_here)
    reach_devices = min(seq_devices - 1, (WINDOW - 2) // blocks_here + 1)
    passing = local_kv
    for hop_index in range(reach_devices):
        passing = passed_along(passing, "seq", 1)
        carried = attend(carried, passing, (device_row - hop_index - 1) * blocks_here)
    fine_out = carried[2] / carried[1][..., None]
    mixed_heads = (
        jnp.transpose(branch_gates[:, 0, :])[..., None] * coarse_out
        + jnp.transpose(branch_gates[:, 1, :])[..., None] * fine_out
    )
    hidden_state = (
        jnp.transpose(mixed_heads, (1, 0, 2)).reshape(tokens_here, features).astype(jnp.bfloat16)
    )
    routes_per = expert_ids.shape[1]
    capacity = 5 * tokens_here * routes_per // (4 * seq_devices)
    flat_ids = expert_ids.reshape(-1)
    onehot = (flat_ids[:, None] == jnp.arange(seq_devices, dtype=jnp.int32)[None, :]).astype(
        jnp.int32
    )
    slot_index = jnp.sum((jnp.cumsum(onehot, axis=0) - 1) * onehot, axis=1)
    destination = flat_ids * capacity + slot_index
    rows_of = jnp.arange(tokens_here * routes_per, dtype=jnp.int32) // routes_per
    outgoing = (
        jnp.zeros((seq_devices * capacity, features), jnp.bfloat16)
        .at[destination]
        .set(hidden_state[rows_of])
    )
    outgoing = outgoing.reshape(seq_devices, capacity, features)
    arrived = lax.all_to_all(outgoing, "seq", split_axis=0, concat_axis=0, tiled=True)
    sources = arrived.shape[0]
    slots = arrived.shape[1]
    wide_rows = arrived.reshape(sources * slots, features).astype(jnp.float32)
    squares = jnp.sum(wide_rows * wide_rows, axis=1)
    normed = (wide_rows * norm_gain).astype(jnp.bfloat16)
    partials = jnp.einsum("rd,dgh->rgh", normed, w_gate_up[0], preferred_element_type=jnp.float32)
    spread = jnp.broadcast_to(squares[:, None], (squares.shape[0], lax.axis_size("exp")))
    summed = lax.psum_scatter(
        partials.astype(jnp.bfloat16), "exp", scatter_dimension=2, tiled=True
    ).astype(jnp.float32)
    square_share = lax.psum_scatter(
        spread.astype(jnp.bfloat16), "exp", scatter_dimension=1, tiled=True
    ).astype(jnp.float32)
    row_scale = lax.rsqrt(square_share[:, 0] / D + EPSILON)[:, None]
    activated = (jax.nn.silu(summed[:, 0] * row_scale) * (summed[:, 1] * row_scale)).astype(
        jnp.bfloat16
    )
    down_rows = w_down[0]
    result = jnp.dot(
        lax.all_gather(activated, "exp", axis=1, tiled=True),
        down_rows,
        preferred_element_type=jnp.float32,
    )
    results_here = result.astype(jnp.bfloat16).reshape(sources, slots, features)
    returned = lax.all_to_all(results_here, "seq", split_axis=0, concat_axis=0, tiled=True)
    flattened = returned.reshape(seq_devices * capacity, features)
    picked_rows = flattened[destination].reshape(tokens_here, routes_per, features)
    route_weight = ROUTE_SCALE * route_scores / jnp.sum(route_scores, axis=1, keepdims=True)
    routed = jnp.einsum("tk,tkd->td", route_weight, picked_rows.astype(jnp.float32))
    return (hidden_state.astype(jnp.float32) + routed).astype(jnp.bfloat16)


def solution(mesh):
    placed = (
        P("seq", "exp"),
        P("seq", "exp"),
        P("seq", "exp"),
        P("seq", None, "exp"),
        P("seq", None),
        P("exp"),
        P("seq", None),
        P("seq", None),
        P("seq", "exp", None, None),
        P("seq", None, "exp"),
    )
    return jax.shard_map(
        local, mesh=mesh, in_specs=placed, out_specs=P("seq", "exp"), check_vma=False
    )
```

profile of v0, /device:TPU:28, one launch (start us, length us, event | category | flops | bytes accessed | tf_op | source)
XLA Modules:
  0.0 925.1 jit_solution(3243886218123410287)
XLA Ops:
  6.5 1.6 copy.181
  10.2 3.5 collective-permute-start
  15.8 4.5 reduce-window.6
  20.8 34.4 %collective-permute-done = bf16[2,128,3584]{1,2,0:T(8,128)(2,1)} collective-permute-done((bf16[2,128,3584]{1,2,0:T(8,128)(2,1)}, bf16[2,128,3584]{1,2,0:T(8,128)(2,1)}, u32[]{:S(2)}, u32[]{:S(2)}) %collective-permute-start) | collective-permute-done | bytes 1835040 | tf_op jit(solution)/shard_map/ppermute | solution.py:20
  55.2 2.5 collective-permute-start.1
  59.3 68.8 %all_gather.6 = bf16[2,32,3584]{2,0,1:T(2,128)(2,1)S(1)} all-gather(bf16[2,2,3584]{2,0,1:T(2,128)(2,1)S(1)} %copy.174), channel_id=1, replica_groups=mesh['seq'=16,'exp'=2] {'seq'}, dimensions={1}, use_global_device_ids=true | all-gather | bytes 487424 | tf_op jit(solution)/shard_map/all_gather | solution.py:51
  128.3 1.9 slice_reduce_fusion
  130.2 4.2 collective-permute-start.2
  138.3 32.1 %collective-permute-done.2 = bf16[2,128,3584]{1,2,0:T(8,128)(2,1)} collective-permute-done((bf16[2,128,3584]{1,2,0:T(8,128)(2,1)}, bf16[2,128,3584]{1,2,0:T(8,128)(2,1)}, u32[]{:S(2)}, u32[]{:S(2)}) %collective-permute-start.2) | collective-permute-done | bytes 1835040 | tf_op jit(solution)/shard_map/ppermute | solution.py:20
  170.4 4.2 collective-permute-start.3
  177.2 33.6 %collective-permute-done.3 = bf16[2,128,3584]{1,2,0:T(8,128)(2,1)S(1)} collective-permute-done((bf16[2,128,3584]{1,2,0:T(8,128)(2,1)}, bf16[2,128,3584]{1,2,0:T(8,128)(2,1)S(1)}, u32[]{:S(2)}, u32[]{:S(2)}) %collective-permute-start.3) | collective-permute-done | bytes 1835040 | tf_op jit(solution)/shard_map/ppermute | solution.py:20
  210.8 4.2 collective-permute-start.4
  218.7 32.3 %collective-permute-done.4 = bf16[2,128,3584]{1,2,0:T(8,128)(2,1)S(1)} collective-permute-done((bf16[2,128,3584]{1,2,0:T(8,128)(2,1)S(1)}, bf16[2,128,3584]{1,2,0:T(8,128)(2,1)S(1)}, u32[]{:S(2)}, u32[]{:S(2)}) %collective-permute-start.4) | collective-permute-done | bytes 1835040 | tf_op jit(solution)/shard_map/ppermute | solution.py:20
  251.0 4.2 collective-permute-start.5
  256.4 34.8 %collective-permute-done.5 = bf16[2,128,3584]{1,2,0:T(8,128)(2,1)S(1)} collective-permute-done((bf16[2,128,3584]{1,2,0:T(8,128)(2,1)S(1)}, bf16[2,128,3584]{1,2,0:T(8,128)(2,1)S(1)}, u32[]{:S(2)}, u32[]{:S(2)}) %collective-permute-start.5) | collective-permute-done | bytes 1835040 | tf_op jit(solution)/shard_map/ppermute | solution.py:20
  291.2 4.7 collective-permute-start.6
  297.2 29.3 %collective-permute-done.6 = bf16[2,128,3584]{1,2,0:T(8,128)(2,1)S(1)} collective-permute-done((bf16[2,128,3584]{1,2,0:T(8,128)(2,1)S(1)}, bf16[2,128,3584]{1,2,0:T(8,128)(2,1)S(1)}, u32[]{:S(2)}, u32[]{:S(2)}) %collective-permute-start.6) | collective-permute-done | bytes 1835040 | tf_op jit(solution)/shard_map/ppermute | solution.py:20
  333.8 1.8 fusion.50
  336.2 37.8 %scatter_custom_fusion = bf16[1280,3584]{1,0:T(8,128)(2,1)} fusion(s32[1024]{0:T(1024)S(1)} %bitcast.450, bf16[128,3584]{1,0:T(8,128)(2,1)S(1)} %copy.217, s32[1024]{0:T(1024)S(1)} %broadcast_clamp_fusion.1, bf16[]{:T(256)} %constant.167.clone.1), kind=kCustom, calls=%fused_computation.14 | custom fusion | bytes 9175042 | tf_op jit(solution)/shard_map/scatter | solution.py:134
  374.0 196.8 %all_to_all.10 = bf16[16,80,3584]{2,1,0:T(8,128)(2,1)} all-to-all(bf16[16,80,3584]{2,1,0:T(8,128)(2,1)} %bitcast.422), channel_id=1, replica_groups=mesh['seq'=16,'exp'=2] {'seq'}, dimensions={0} | all-to-all | bytes 18350080 | tf_op jit(solution)/shard_map/all_to_all | solution.py:137
  570.9 12.3 %fusion.3 = (bf16[16,80]{1,0:T(8,128)(2,1)S(1)}, bf16[16,80,3584]{2,1,0:T(8,128)(2,1)}) fusion(bf16[16,80,3584]{2,1,0:T(8,128)(2,1)} %all_to_all.10, f32[3584]{0:T(1024)S(1)} %copy-done.4), kind=kLoop, calls=%fused_computation.8 | loop fusion | flops 22936320 | bytes 18366976 | tf_op jit(solution)/shard_map/reduce_sum | solution.py:141
  583.1 36.4 %fusion.5 = bf16[1280,2,1536]{2,0,1:T(8,128)(2,1)} fusion(bf16[1280,3584,1]{1,0,2:T(8,128)(2,1)} %bitcast.424, bf16[3584,2,1536]{2,1,0:T(2,128)(2,1)} %bitcast.453), kind=kOutput, calls=%fused_computation.11 | convolution fusion | flops 28189655040 | bytes 39059456 | tf_op jit(solution)/shard_map/rd,dgh->rgh/dot_general | solution.py:143
  620.9 2.5 all-reduce
  624.0 12.4 %reduce-scatter.2.cloned.1.call-done = bf16[1280,2,768]{2,0,1:T(8,128)(2,1)} async-done(((bf16[1280,2,1536]{2,0,1:T(8,128)(2,1)}), bf16[1280,2,768]{2,0,1:T(8,128)(2,1)}) %reduce-scatter.2.cloned.1.call-update) | async-done | bytes 3932176 | tf_op jit(solution)/shard_map/reduce_scatter | solution.py:145
  636.5 2.7 convert_element_type.104
  639.2 2.7 fusion.15
  641.9 14.6 %all-gather.2.cloned.1.call-done = bf16[1280,1536]{1,0:T(8,128)(2,1)} async-done(((bf16[1280,768]{1,0:T(8,128)(2,1)}), bf16[1280,1536]{1,0:T(8,128)(2,1)}) %all-gather.2.cloned.1.call-update) | async-done | bytes 3932176 | tf_op jit(solution)/shard_map/all_gather | solution.py:157
  656.5 20.5 %convolution_convert_fusion = bf16[1280,3584]{1,0:T(8,128)(2,1)} fusion(bf16[1280,1536]{1,0:T(8,128)(2,1)} %all-gather.2.cloned.1.call-done, bf16[1,1536,3584]{2,1,0:T(8,128)(2,1)} %param.19), kind=kOutput, calls=%fused_computation.9 | convolution fusion | flops 14097448960 | bytes 24117248 | tf_op jit(solution)/shard_map/dot_general | solution.py:156
  677.0 7.4 all-to-all-start.1
  684.6 208.6 %all-to-all-done.1 = bf16[16,80,3584]{2,1,0:T(8,128)(2,1)} async-done(((bf16[16,80,3584]{2,1,0:T(8,128)(2,1)}), bf16[16,80,3584]{2,1,0:T(8,128)(2,1)}, u32[]{:S(2)}, u32[]{:S(2)}) %all-to-all-start.1) | async-done | bytes 9175072 | tf_op jit(solution)/shard_map/all_to_all | solution.py:162
  893.2 18.6 %gather_fusion = bf16[1024,3584]{1,0:T(8,128)(2,1)} fusion(bf16[1280,3584]{1,0:T(8,128)(2,1)} %bitcast.73, s32[1024]{0:T(1024)S(1)} %broadcast_clamp_fusion), kind=kCustom, calls=%fused_computation.1 | custom fusion | bytes 14684160 | tf_op jit(solution)/shard_map/gather | solution.py:164
  911.8 5.1 fusion.8
  (119 shorter events, 29.6 us)
Async XLA Ops:
  6.5 1.6 copy-start
  6.5 629.9 %reduce-scatter.2.cloned.1.call-start = ((), (), s32[]{:S(2)}) async-start(), calls=%async_computation.3 | async-start | bytes 11796480 | tf_op jit(solution)/shard_map/reduce_scatter | solution.py:145
  8.8 5.1 copy-start.2
  10.2 47.6 %copy-start.5 = (s32[2,8]{1,0:T(2,128)S(1)}, s32[2,8]{1,0:T(2,128)}, u32[]{:S(2)}) copy-start(s32[2,8]{1,0:T(2,128)} %param.14) | copy-start | bytes 196
  10.2 45.0 %collective-permute-start = (bf16[2,128,3584]{1,2,0:T(8,128)(2,1)}, bf16[2,128,3584]{1,2,0:T(8,128)(2,1)}, u32[]{:S(2)}, u32[]{:S(2)}) collective-permute-start(bf16[2,128,3584]{1,2,0:T(8,128)(2,1)} %pad_maximum_fusion), channel_id=1, source_target_pairs={{0,2},{2,4},{4,6},{6,8},{8,10},{10,12},{12,14},{14,16},{16,18},{18... | collective-permute-start | bytes 5505032 | tf_op jit(solution)/shard_map/ppermute | solution.py:20
  55.2 75.0 %collective-permute-start.1 = (bf16[2,128,3584]{1,2,0:T(8,128)(2,1)}, bf16[2,128,3584]{1,2,0:T(8,128)(2,1)}, u32[]{:S(2)}, u32[]{:S(2)}) collective-permute-start(bf16[2,128,3584]{1,2,0:T(8,128)(2,1)} %collective-permute-done), channel_id=1, source_target_pairs={{0,2},{2,4},{4,6},{6,8},{8,10},{10,12},{12,14},{14,16},{16,18},{18... | collective-permute-start | bytes 5505032 | tf_op jit(solution)/shard_map/ppermute | solution.py:20
  130.2 40.2 %collective-permute-start.2 = (bf16[2,128,3584]{1,2,0:T(8,128)(2,1)}, bf16[2,128,3584]{1,2,0:T(8,128)(2,1)}, u32[]{:S(2)}, u32[]{:S(2)}) collective-permute-start(bf16[2,128,3584]{1,2,0:T(8,128)(2,1)} %collective-permute-done.1), channel_id=1, source_target_pairs={{0,2},{2,4},{4,6},{6,8},{8,10},{10,12},{12,14},{14,16},{16,18},{18... | collective-permute-start | bytes 5505032 | tf_op jit(solution)/shard_map/ppermute | solution.py:20
  134.6 3.2 copy-start.1
  170.4 40.4 %collective-permute-start.3 = (bf16[2,128,3584]{1,2,0:T(8,128)(2,1)}, bf16[2,128,3584]{1,2,0:T(8,128)(2,1)S(1)}, u32[]{:S(2)}, u32[]{:S(2)}) collective-permute-start(bf16[2,128,3584]{1,2,0:T(8,128)(2,1)} %collective-permute-done.2), channel_id=1, source_target_pairs={{0,2},{2,4},{4,6},{6,8},{8,10},{10,12},{12,14},{14,16},{16,18},{18... | collective-permute-start | bytes 5505032 | tf_op jit(solution)/shard_map/ppermute | solution.py:20
  210.8 40.2 %collective-permute-start.4 = (bf16[2,128,3584]{1,2,0:T(8,128)(2,1)S(1)}, bf16[2,128,3584]{1,2,0:T(8,128)(2,1)S(1)}, u32[]{:S(2)}, u32[]{:S(2)}) collective-permute-start(bf16[2,128,3584]{1,2,0:T(8,128)(2,1)S(1)} %collective-permute-done.3), channel_id=1, source_target_pairs={{0,2},{2,4},{4,6},{6,8},{8,10},{10,12},{12,14},{14,16},{16,18},{18... | collective-permute-start | bytes 5505032 | tf_op jit(solution)/shard_map/ppermute | solution.py:20
  251.0 40.2 %collective-permute-start.5 = (bf16[2,128,3584]{1,2,0:T(8,128)(2,1)S(1)}, bf16[2,128,3584]{1,2,0:T(8,128)(2,1)S(1)}, u32[]{:S(2)}, u32[]{:S(2)}) collective-permute-start(bf16[2,128,3584]{1,2,0:T(8,128)(2,1)S(1)} %collective-permute-done.4), channel_id=1, source_target_pairs={{0,2},{2,4},{4,6},{6,8},{8,10},{10,12},{12,14},{14,16},{16,18},{18... | collective-permute-start | bytes 5505032 | tf_op jit(solution)/shard_map/ppermute | solution.py:20
  291.2 35.3 %collective-permute-start.6 = (bf16[2,128,3584]{1,2,0:T(8,128)(2,1)S(1)}, bf16[2,128,3584]{1,2,0:T(8,128)(2,1)S(1)}, u32[]{:S(2)}, u32[]{:S(2)}) collective-permute-start(bf16[2,128,3584]{1,2,0:T(8,128)(2,1)S(1)} %collective-permute-done.5), channel_id=1, source_target_pairs={{0,2},{2,4},{4,6},{6,8},{8,10},{10,12},{12,14},{14,16},{16,18},{18... | collective-permute-start | bytes 5505032 | tf_op jit(solution)/shard_map/ppermute | solution.py:20
  374.0 196.8 %copy-start.4 = (f32[3584]{0:T(1024)S(1)}, f32[3584]{0:T(1024)}, u32[]{:S(2)}) copy-start(f32[3584]{0:T(1024)} %param.15) | copy-start | bytes 43012
  619.5 0.7 copy-start.6
  619.6 37.0 %all-gather.2.cloned.1.call-start = ((), (), s32[]{:S(2)}) async-start(), calls=%async_computation.4 | async-start | bytes 5898240 | tf_op jit(solution)/shard_map/all_gather | solution.py:157
  677.0 7.4 copy-start.3
  677.0 216.2 %all-to-all-start.1 = ((bf16[16,80,3584]{2,1,0:T(8,128)(2,1)}), bf16[16,80,3584]{2,1,0:T(8,128)(2,1)}, u32[]{:S(2)}, u32[]{:S(2)}) async-start(bf16[16,80,3584]{2,1,0:T(8,128)(2,1)} %bitcast.423), calls=%async_computation.2 | async-start | bytes 18350080 | tf_op jit(solution)/shard_map/all_to_all | solution.py:162
Sparse Core Ops, SparseCore 0:
  619.7 16.7 reduce-scatter.1
  642.0 14.4 all-gather.1
where the time goes:
time: 934 us; the launch traced here: 925 us
  waiting for transfers between devices  432 us (46%)
  blocking collectives  268 us (29%)
  matrix products  72 us (8%)
  local copies, waits for them, and re-layouts  71.1 us (8%)
  starting transfers between devices  35 us (4%)
  other arithmetic  32.4 us (3%)
  between operations  14.4 us (2%)
    all_to_all x1, waiting for transfers between devices, local(): lax.all_to_all(results_here, 'seq', split_axis=0, concat_axis=0, tiled=True)  209 us
    all_to_all x1, blocking collectives, local(): lax.all_to_all(outgoing, 'seq', split_axis=0, concat_axis=0, tiled=True)  197 us
    ppermute x7, waiting for transfers between devices, passed_along(): return lax.ppermute(shard, axis, pairs)  196 us
    all_gather x1, blocking collectives, local(): everyone = lax.all_gather(pooled, 'seq', axis=1, tiled=True)  68.8 us
    scatter x1, local copies, waits for them, and re-layouts, local(): outgoing = jnp.zeros((seq_devices * capacity, features), jnp.bfloat16).at...  37.8 us
    dot_general x1, matrix products, local(): jnp.einsum('rd,dgh->rgh', normed, w_gate_up[0], preferred_element_type=jn...  36.4 us
    ppermute x7, starting transfers between devices, passed_along(): return lax.ppermute(shard, axis, pairs)  27.6 us
    dot_general x1, matrix products, local(): jnp.dot(lax.all_gather(activated, 'exp', axis=1, tiled=True), down_rows,...  20.5 us
  transfers between devices with their start and end apart: 10, of which 9 were waited for; matrix products, arithmetic and copies ran while one was open for 3% of the time, Pallas kernels for 0%

commit v1 on v0

v1 whole, which is shorter than its diff:
```python
import functools

import jax
import jax.numpy as jnp
from jax import lax
from jax.experimental import pallas as pl
from jax.experimental.pallas import tpu as pltpu
from jax.sharding import PartitionSpec as P

HD = 128
D = 7168
BLOCK = 64
WINDOW = 15


EPSILON = 1e-06
ROUTE_SCALE = 2.5
MASKED_SCORE = -1e30


def pieces(x):
    out = []
    for _ in range(3):
        part = lax.reduce_precision(x, 8, 7)
        out.append(part.astype(jnp.bfloat16))
        x = x - part
    return jnp.stack(out)


def attention_kernel(
    heads, window, q_ref, k_ref, v_ref, pk_ref, pv_ref, bias_ref, gate_ref, out_ref
):
    tile = q_ref.shape[0]
    step = pl.program_id(0)
    scale = HD ** (-0.5)
    start = pl.multiple_of(step * tile, tile)
    blocks = pk_ref.shape[0]
    bias = bias_ref[...].astype(jnp.float32)
    row = lax.broadcasted_iota(jnp.int32, (tile, blocks), 0)
    column = lax.broadcasted_iota(jnp.int32, (tile, blocks), 1)
    earlier = column < step * (tile // BLOCK) + row // BLOCK
    gates = gate_ref[...]
    contract = (((1,), (1,)), ((), ()))
    for h in range(heads):
        lanes = slice(h * HD, (h + 1) * HD)
        q = q_ref[:, lanes]
        s = lax.dot_general(
            q, k_ref[pl.ds(start, window), lanes], contract, preferred_element_type=jnp.float32
        )
        s = s * scale + bias
        m = jnp.max(s, axis=1, keepdims=True)
        w = jnp.exp(s - m)
        den = jnp.sum(w, axis=1, keepdims=True)
        fine = jnp.dot(
            w.astype(jnp.bfloat16),
            v_ref[pl.ds(start, window), lanes],
            preferred_element_type=jnp.float32,
        )
        sc = lax.dot_general(q, pk_ref[:, lanes], contract, preferred_element_type=jnp.float32)
        sc = jnp.where(earlier, sc * scale, MASKED_SCORE)
        mc = jnp.max(sc, axis=1, keepdims=True)
        mc = jnp.where(mc > 0.5 * MASKED_SCORE, mc, 0.0)
        wc = jnp.where(earlier, jnp.exp(sc - mc), 0.0)
        dc = jnp.maximum(jnp.sum(wc, axis=1, keepdims=True), 1.0)
        coarse = jnp.dot(
            wc.astype(jnp.bfloat16), pv_ref[:, lanes], preferred_element_type=jnp.float32
        )
        g0 = gates[:, h : h + 1]
        g1 = gates[:, heads + h : heads + h + 1]
        out_ref[:, lanes] = (coarse * (g0 / dc) + fine * (g1 / den)).astype(jnp.bfloat16)


def attention(queries, keys, values, branch_gates, block_choice):
    tokens, features = queries.shape
    seq = lax.axis_size("seq")
    heads_here = features // HD
    heads = -(-heads_here // seq)
    width = heads * HD
    blocks_here = tokens // BLOCK
    pad = seq * heads - heads_here

    def dealt(x):
        x = jnp.pad(x, ((0, 0), (0, pad * HD)))
        return jnp.transpose(x.reshape(tokens, seq, width), (1, 0, 2))

    gates = jnp.pad(branch_gates, ((0, 0), (0, 0), (0, pad)))
    gates = pieces(gates.reshape(tokens, 2, seq, heads))
    gates = jnp.transpose(gates, (3, 0, 2, 4, 1)).reshape(seq, -1)
    choice = jnp.broadcast_to(block_choice.reshape(1, -1), (seq, block_choice.size))
    extra = jnp.concatenate([gates, choice.astype(jnp.bfloat16)], axis=1)
    rows = -(-extra.shape[1] // (16 * width)) * 16
    extra = jnp.pad(extra, ((0, 0), (0, rows * width - extra.shape[1])))
    packed = jnp.concatenate(
        [dealt(queries), dealt(keys), dealt(values), extra.reshape(seq, rows, width)], axis=1
    )
    got = lax.all_to_all(packed, "seq", split_axis=0, concat_axis=0, tiled=True)
    q, k, v = (
        got[:, n * tokens : (n + 1) * tokens].reshape(seq * tokens, width) for n in range(3)
    )
    extra = got[:, 3 * tokens :].reshape(seq, rows * width).astype(jnp.float32)
    count = 6 * heads * tokens
    gates = jnp.sum(extra[:, :count].reshape(seq, 3, 2 * heads, tokens), axis=1)
    gates = jnp.transpose(gates, (0, 2, 1)).reshape(seq * tokens, 2 * heads)
    choice = extra[:, count : count + block_choice.size].astype(jnp.int32)
    choice = choice.reshape(seq, blocks_here, 1, block_choice.shape[1])

    before = (WINDOW - 1) * BLOCK
    window = before + tokens
    window_blocks = window // BLOCK
    gap = (
        jnp.arange(blocks_here, dtype=jnp.int32)[:, None]
        + (WINDOW - 1)
        - jnp.arange(window_blocks, dtype=jnp.int32)[None, :]
    )
    chosen = jnp.any(choice == gap[None, :, :, None], axis=3)
    inside = (
        jnp.arange(seq, dtype=jnp.int32)[:, None] * blocks_here
        + jnp.arange(window_blocks, dtype=jnp.int32)[None, :]
        >= WINDOW - 1
    )
    chosen = chosen & inside[:, None, :]
    chosen = jnp.broadcast_to(
        chosen[:, :, None, :, None], (seq, blocks_here, BLOCK, window_blocks, BLOCK)
    ).reshape(seq, tokens, window)
    causal = (
        jnp.arange(window, dtype=jnp.int32)[None, :] - before
        <= jnp.arange(tokens, dtype=jnp.int32)[:, None]
    )
    bias = jnp.where(chosen & causal[None], 0.0, MASKED_SCORE).astype(jnp.bfloat16)
    bias = bias.reshape(seq * tokens, window)

    def pooled(x):
        x = x.astype(jnp.float32).reshape(seq * blocks_here, BLOCK, width)
        return jnp.mean(x, axis=1).astype(jnp.bfloat16)

    def whole(x):
        return pl.BlockSpec(x.shape, lambda i: (0,) * x.ndim)

    pk, pv = pooled(k), pooled(v)
    kp = jnp.pad(k, ((before, 0), (0, 0)))
    vp = jnp.pad(v, ((before, 0), (0, 0)))
    out = pl.pallas_call(
        functools.partial(attention_kernel, heads, window),
        grid=(seq,),
        out_shape=jax.ShapeDtypeStruct((seq * tokens, width), jnp.bfloat16),
        in_specs=[
            pl.BlockSpec((tokens, width), lambda i: (i, 0)),
            whole(kp),
            whole(vp),
            whole(pk),
            whole(pv),
            pl.BlockSpec((tokens, window), lambda i: (i, 0)),
            pl.BlockSpec((tokens, 2 * heads), lambda i: (i, 0)),
        ],
        out_specs=pl.BlockSpec((tokens, width), lambda i: (i, 0)),
        compiler_params=pltpu.CompilerParams(vmem_limit_bytes=40 * 1024 * 1024),
    )(q, kp, vp, pk, pv, bias, gates)
    back = lax.all_to_all(
        out.reshape(seq, tokens, width), "seq", split_axis=0, concat_axis=0, tiled=True
    )
    return jnp.transpose(back, (1, 0, 2)).reshape(tokens, seq * width)[:, :features]


def local(
    queries,
    keys,
    values,
    branch_gates,
    block_choice,
    norm_gain,
    expert_ids,
    route_scores,
    w_gate_up,
    w_down,
):
    tokens_here, features = queries.shape
    seq_devices = lax.axis_size("seq")
    routes_per = expert_ids.shape[1]
    capacity = 5 * tokens_here * routes_per // (4 * seq_devices)
    named = expert_ids[:, :, None] == jnp.arange(seq_devices, dtype=jnp.int32)[None, None, :]
    member = jnp.any(named, axis=1)
    before = jnp.tri(tokens_here, k=-1, dtype=jnp.bfloat16)
    slot = jnp.dot(before, member.astype(jnp.bfloat16), preferred_element_type=jnp.float32)
    slot = jnp.where(member, slot.astype(jnp.int32), -1)
    places = jnp.arange(capacity, dtype=jnp.int32)
    at_slot = jnp.transpose(slot)[:, None, :] == places[None, :, None]
    dispatch = at_slot.astype(jnp.bfloat16).reshape(seq_devices * capacity, tokens_here)
    route_weight = ROUTE_SCALE * route_scores / jnp.sum(route_scores, axis=1, keepdims=True)
    weight = jnp.sum(jnp.where(named, route_weight[:, :, None], 0.0), axis=1)
    back_to = slot[:, :, None] == places[None, None, :]
    weight_parts = pieces(weight)[:2]
    combine = jnp.where(back_to[None], weight_parts[..., None], jnp.bfloat16(0)).reshape(
        2, tokens_here, seq_devices * capacity
    )

    hidden_state = attention(queries, keys, values, branch_gates, block_choice)
    outgoing = jnp.dot(dispatch, hidden_state, preferred_element_type=jnp.float32)
    outgoing = outgoing.astype(jnp.bfloat16).reshape(seq_devices, capacity, features)
    arrived = lax.all_to_all(outgoing, "seq", split_axis=0, concat_axis=0, tiled=True)
    sources = arrived.shape[0]
    slots = arrived.shape[1]
    wide_rows = arrived.reshape(sources * slots, features).astype(jnp.float32)
    squares = jnp.sum(wide_rows * wide_rows, axis=1)
    normed = (wide_rows * norm_gain).astype(jnp.bfloat16)
    partials = jnp.einsum("rd,dgh->rgh", normed, w_gate_up[0], preferred_element_type=jnp.float32)
    spread = jnp.broadcast_to(squares[:, None], (squares.shape[0], lax.axis_size("exp")))
    summed = lax.psum_scatter(
        partials.astype(jnp.bfloat16), "exp", scatter_dimension=2, tiled=True
    ).astype(jnp.float32)
    square_share = lax.psum_scatter(
        spread.astype(jnp.bfloat16), "exp", scatter_dimension=1, tiled=True
    ).astype(jnp.float32)
    row_scale = lax.rsqrt(square_share[:, 0] / D + EPSILON)[:, None]
    activated = (jax.nn.silu(summed[:, 0] * row_scale) * (summed[:, 1] * row_scale)).astype(
        jnp.bfloat16
    )
    down_rows = w_down[0]
    result = jnp.dot(
        lax.all_gather(activated, "exp", axis=1, tiled=True),
        down_rows,
        preferred_element_type=jnp.float32,
    )
    results_here = result.astype(jnp.bfloat16).reshape(sources, slots, features)
    returned = lax.all_to_all(results_here, "seq", split_axis=0, concat_axis=0, tiled=True)
    flattened = returned.reshape(seq_devices * capacity, features)
    routed = jnp.dot(combine[0], flattened, preferred_element_type=jnp.float32) + jnp.dot(
        combine[1], flattened, preferred_element_type=jnp.float32
    )
    return (hidden_state.astype(jnp.float32) + routed).astype(jnp.bfloat16)


def solution(mesh):
    placed = (
        P("seq", "exp"),
        P("seq", "exp"),
        P("seq", "exp"),
        P("seq", None, "exp"),
        P("seq", None),
        P("exp"),
        P("seq", None),
        P("seq", None),
        P("seq", "exp", None, None),
        P("seq", None, "exp"),
    )
    return jax.shard_map(
        local, mesh=mesh, in_specs=placed, out_specs=P("seq", "exp"), check_vma=False
    )
```

time: 934 us -> 721 us (0.77)
  waiting for transfers between devices: 432 us -> 330 us
  blocking collectives: 268 us -> 205 us
  local copies, waits for them, and re-layouts: 71.1 us -> 29 us
  Pallas kernels: 0 us -> 22.4 us
  starting transfers between devices: 35 us -> 20.3 us
    ppermute x7 -> x0, waiting for transfers between devices: 196 us -> none  [passed_along(): return lax.ppermute(shard, axis, pairs)]
    all_to_all x0 -> x2, waiting for transfers between devices: none -> 94.6 us  [the longest x1 71.7 us: attention(): got = lax.all_to_all(packed, 'seq', split_axis=0, concat_axis=0, tiled=True)]
    all_gather x1 -> x0, blocking collectives: 68.8 us -> none  [local(): everyone = lax.all_gather(pooled, 'seq', axis=1, tiled=True)]
    scatter x1 -> x0, local copies, waits for them, and re-layouts: 37.8 us -> none  [local(): outgoing = jnp.zeros((seq_devices * capacity, features), jnp.bfloat16).at...]
    ppermute x7 -> x0, starting transfers between devices: 27.6 us -> none  [passed_along(): return lax.ppermute(shard, axis, pairs)]
    pallas_call x0 -> x1, Pallas kernels: none -> 22.4 us  [attention(): pl.pallas_call(functools.partial(attention_kernel, heads, window), grid=(...]
    gather x1 -> x0, local copies, waits for them, and re-layouts: 18.6 us -> none  [local(): flattened[destination].reshape(tokens_here, routes_per, features)]
    all_to_all x0 -> x2, starting transfers between devices: none -> 13.2 us  [the longest x1 6.94 us: attention(): got = lax.all_to_all(packed, 'seq', split_axis=0, concat_axis=0, tiled=True)]
  transfers between devices with their start and end apart: 10 -> 5, of which waited for: 9 -> 5; matrix products, arithmetic and copies ran while one was open for 3% -> 0% of each run, Pallas kernels for 0% -> 0%
where the time goes in v1:
time: 721 us; the launch traced here: 719 us
  waiting for transfers between devices  330 us (46%)
  blocking collectives  205 us (28%)
  matrix products  70.6 us (10%)
  local copies, waits for them, and re-layouts  29 us (4%)
  other arithmetic  27.6 us (4%)
  Pallas kernels  22.4 us (3%)
  starting transfers between devices  20.3 us (3%)
  between operations  13.8 us (2%)
    all_to_all x1, waiting for transfers between devices, local(): lax.all_to_all(results_here, 'seq', split_axis=0, concat_axis=0, tiled=True)  209 us
    all_to_all x1, blocking collectives, local(): lax.all_to_all(outgoing, 'seq', split_axis=0, concat_axis=0, tiled=True)  203 us
    all_to_all x1, waiting for transfers between devices, attention(): got = lax.all_to_all(packed, 'seq', split_axis=0, concat_axis=0, tiled=True)  71.7 us
    dot_general x1, matrix products, local(): jnp.einsum('rd,dgh->rgh', normed, w_gate_up[0], preferred_element_type=jn...  36.4 us
    all_to_all x1, waiting for transfers between devices, attention(): lax.all_to_all(out.reshape(seq, tokens, width), 'seq', split_axis=0, conc...  22.8 us
    pallas_call x1, Pallas kernels, attention(): pl.pallas_call(functools.partial(attention_kernel, heads, window), grid=(...  22.4 us
    dot_general x1, matrix products, local(): jnp.dot(lax.all_gather(activated, 'exp', axis=1, tiled=True), down_rows,...  20.5 us
    all_gather x1, waiting for transfers between devices, local(): lax.all_gather(activated, 'exp', axis=1, tiled=True)  14.6 us
  transfers between devices with their start and end apart: 5, of which 5 were waited for; matrix products, arithmetic and copies ran while one was open for 0% of the time, Pallas kernels for 0%

profile of v1, /device:TPU:28, one launch (start us, length us, event | category | flops | bytes accessed | tf_op | source)
XLA Modules:
  0.0 719.4 jit_solution(5765615333816433072)
XLA Ops:
  8.3 1.3 pad.26
  9.6 1.3 pad.27
  10.8 1.3 pad.25
  12.5 1.8 pad_maximum_fusion
  14.3 6.9 all-to-all-start
  22.2 71.7 %all-to-all-done = bf16[16,400,256]{2,1,0:T(8,128)(2,1)S(1)} async-done(((bf16[16,400,256]{2,1,0:T(8,128)(2,1)}), bf16[16,400,256]{2,1,0:T(8,128)(2,1)S(1)}, u32[]{:S(2)}, u32[]{:S(2)}) %all-to-all-start) | async-done | bytes 3276832 | tf_op jit(solution)/shard_map/all_to_all | solution.py:96
  93.9 2.0 copy.68
  96.6 2.1 slice.51
  98.6 1.3 fusion.25
  100.9 3.1 broadcast_in_dim.49
  103.9 10.8 %reshape.257 = pred[2048,1024]{1,0:T(8,128)(4,1)} reshape(pred[16,2,64,16,64]{4,3,2,1,0:T(8,128)(4,1)} %broadcast_in_dim.49) | data formatting | bytes 4194304 | tf_op jit(solution)/shard_map/reshape | solution.py:124
  114.7 1.2 reduce_sum.58
  115.9 1.9 copy.70
  117.9 3.0 select_convert_fusion.bias_ref
  121.0 22.4 %shard_map.100 = bf16[2048,256]{1,0:T(8,128)(2,1)S(1)} custom-call(bf16[2048,256]{1,0:T(8,128)(2,1)S(1)} %bitcast.88, bf16[2944,256]{1,0:T(8,128)(2,1)S(1)} %pad.30.k_ref, bf16[2944,256]{1,0:T(8,128)(2,1)S(1)} %pad.31.v_ref, bf16[32,256]{1,0:T(8,128)(2,1)S(1)} %multiply_convert_fusion.1.pk_ref, bf16[32,256]{1,0:T(8,128)(2,1)S(1)} %multiply_convert_fusion.pv_ref, ...), custom_call_target="tpu_custom_call" | custom-call | tf_op jit(solution)/shard_map/pallas_call | solution.py:142
  143.4 1.0 copy-done.1
  144.3 6.2 all-to-all-start.1
  151.2 22.8 %all-to-all-done.1 = bf16[16,128,256]{2,1,0:T(8,128)(2,1)S(1)} async-done(((bf16[16,128,256]{2,1,0:T(8,128)(2,1)}), bf16[16,128,256]{2,1,0:T(8,128)(2,1)S(1)}, u32[]{:S(2)}, u32[]{:S(2)}) %all-to-all-start.1) | async-done | bytes 1048608 | tf_op jit(solution)/shard_map/all_to_all | solution.py:158
  174.1 2.5 convolution_convert_fusion.1
  176.7 202.9 %all_to_all.20 = bf16[16,80,3584]{2,1,0:T(8,128)(2,1)} all-to-all(bf16[16,80,3584]{2,1,0:T(8,128)(2,1)S(1)} %bitcast.89), channel_id=1, replica_groups=mesh['seq'=16,'exp'=2] {'seq'}, dimensions={0} | all-to-all | bytes 18350080 | tf_op jit(solution)/shard_map/all_to_all | solution.py:199
  379.6 12.2 %fusion.3 = (bf16[16,80]{1,0:T(8,128)(2,1)S(1)}, bf16[16,80,3584]{2,1,0:T(8,128)(2,1)}) fusion(bf16[16,80,3584]{2,1,0:T(8,128)(2,1)} %all_to_all.20, f32[3584]{0:T(1024)S(1)} %copy-done.6), kind=kLoop, calls=%fused_computation.5 | loop fusion | flops 22936320 | bytes 18366976 | tf_op jit(solution)/shard_map/reduce_sum | solution.py:203
  391.8 36.4 %fusion.5 = bf16[1280,2,1536]{2,0,1:T(8,128)(2,1)} fusion(bf16[1280,3584,1]{1,0,2:T(8,128)(2,1)} %bitcast.95, bf16[3584,2,1536]{2,1,0:T(2,128)(2,1)} %bitcast.113), kind=kOutput, calls=%fused_computation.9 | convolution fusion | flops 28189655040 | bytes 39059456 | tf_op jit(solution)/shard_map/rd,dgh->rgh/dot_general | solution.py:205
  429.6 2.5 all-reduce.7
  432.7 12.4 %reduce-scatter.2.cloned.1.call-done = bf16[1280,2,768]{2,0,1:T(8,128)(2,1)} async-done(((bf16[1280,2,1536]{2,0,1:T(8,128)(2,1)}), bf16[1280,2,768]{2,0,1:T(8,128)(2,1)}) %reduce-scatter.2.cloned.1.call-update) | async-done | bytes 3932176 | tf_op jit(solution)/shard_map/reduce_scatter | solution.py:207
  445.2 2.7 convert_element_type.175
  447.9 2.5 fusion.12
  450.4 14.6 %all-gather.2.cloned.1.call-done = bf16[1280,1536]{1,0:T(8,128)(2,1)} async-done(((bf16[1280,768]{1,0:T(8,128)(2,1)}), bf16[1280,1536]{1,0:T(8,128)(2,1)}) %all-gather.2.cloned.1.call-update) | async-done | bytes 3932176 | tf_op jit(solution)/shard_map/all_gather | solution.py:219
  465.1 20.5 %convolution_convert_fusion = bf16[1280,3584]{1,0:T(8,128)(2,1)} fusion(bf16[1280,1536]{1,0:T(8,128)(2,1)} %all-gather.2.cloned.1.call-done, bf16[1,1536,3584]{2,1,0:T(8,128)(2,1)} %param.19), kind=kOutput, calls=%fused_computation.6 | convolution fusion | flops 14097448960 | bytes 24117248 | tf_op jit(solution)/shard_map/dot_general | solution.py:218
  485.6 7.1 all-to-all-start.3
  493.0 208.7 %all-to-all-done.3 = bf16[16,80,3584]{2,1,0:T(8,128)(2,1)} async-done(((bf16[16,80,3584]{2,1,0:T(8,128)(2,1)}), bf16[16,80,3584]{2,1,0:T(8,128)(2,1)}, u32[]{:S(2)}, u32[]{:S(2)}) %all-to-all-start.3) | async-done | bytes 9175072 | tf_op jit(solution)/shard_map/all_to_all | solution.py:224
  701.6 5.0 fusion.27
  706.6 6.0 fusion.9
  (69 shorter events, 7.5 us)
Async XLA Ops:
  14.3 79.6 %all-to-all-start = ((bf16[16,400,256]{2,1,0:T(8,128)(2,1)}), bf16[16,400,256]{2,1,0:T(8,128)(2,1)S(1)}, u32[]{:S(2)}, u32[]{:S(2)}) async-start(bf16[16,400,256]{2,1,0:T(8,128)(2,1)} %pad_maximum_fusion), calls=%async_computation | async-start | bytes 6553600 | tf_op jit(solution)/shard_map/all_to_all | solution.py:96
  100.6 17.3 %copy-start.3 = (pred[128,1024]{1,0:T(8,128)(4,1)S(1)}, pred[128,1024]{1,0:T(8,128)(4,1)}, u32[]{:S(2)}) copy-start(pred[128,1024]{1,0:T(8,128)(4,1)} %iota_compare_fusion.1) | copy-start | bytes 393220
  117.9 3.1 copy-start
  117.9 3.1 copy-start.2
  120.9 29.8 %copy-start.5 = (s32[128,8]{0,1:T(8,128)S(1)}, s32[128,8]{0,1:T(8,128)}, u32[]{:S(2)}) copy-start(s32[128,8]{0,1:T(8,128)} %param.16) | copy-start | bytes 12292
  143.4 1.0 copy-start.1
  144.3 29.7 %all-to-all-start.1 = ((bf16[16,128,256]{2,1,0:T(8,128)(2,1)}), bf16[16,128,256]{2,1,0:T(8,128)(2,1)S(1)}, u32[]{:S(2)}, u32[]{:S(2)}) async-start(bf16[16,128,256]{2,1,0:T(8,128)(2,1)} %bitcast.87), calls=%async_computation.1 | async-start | bytes 2097152 | tf_op jit(solution)/shard_map/all_to_all | solution.py:158
  150.6 294.6 %reduce-scatter.2.cloned.1.call-start = ((), (), s32[]{:S(2)}) async-start(), calls=%async_computation.5 | async-start | bytes 11796480 | tf_op jit(solution)/shard_map/reduce_scatter | solution.py:207
  176.7 202.9 %copy-start.6 = (f32[3584]{0:T(1024)S(1)}, f32[3584]{0:T(1024)}, u32[]{:S(2)}) copy-start(f32[3584]{0:T(1024)} %param.15) | copy-start | bytes 43012
  428.2 0.7 copy-start.7
  428.3 36.8 %all-gather.2.cloned.1.call-start = ((), (), s32[]{:S(2)}) async-start(), calls=%async_computation.6 | async-start | bytes 5898240 | tf_op jit(solution)/shard_map/all_gather | solution.py:219
  485.6 7.1 copy-start.4
  485.6 216.1 %all-to-all-start.3 = ((bf16[16,80,3584]{2,1,0:T(8,128)(2,1)}), bf16[16,80,3584]{2,1,0:T(8,128)(2,1)}, u32[]{:S(2)}, u32[]{:S(2)}) async-start(bf16[16,80,3584]{2,1,0:T(8,128)(2,1)} %bitcast.94), calls=%async_computation.4 | async-start | bytes 18350080 | tf_op jit(solution)/shard_map/all_to_all | solution.py:224
Sparse Core Ops, SparseCore 0:
  428.4 16.7 reduce-scatter.1
  450.6 14.4 all-gather.1

commit v2 on v1

--- a/solution.py
+++ b/solution.py
@@ -119,14 +119,23 @@
         >= WINDOW - 1
     )
     chosen = chosen & inside[:, None, :]
+    expand = (
+        jnp.arange(window_blocks, dtype=jnp.int32)[:, None]
+        == jnp.arange(window, dtype=jnp.int32)[None, :] // BLOCK
+    ).astype(jnp.bfloat16)
+    chosen = jnp.dot(
+        chosen.reshape(seq * blocks_here, window_blocks).astype(jnp.bfloat16),
+        expand,
+        preferred_element_type=jnp.float32,
+    )
     chosen = jnp.broadcast_to(
-        chosen[:, :, None, :, None], (seq, blocks_here, BLOCK, window_blocks, BLOCK)
+        chosen.reshape(seq, blocks_here, 1, window), (seq, blocks_here, BLOCK, window)
     ).reshape(seq, tokens, window)
     causal = (
         jnp.arange(window, dtype=jnp.int32)[None, :] - before
         <= jnp.arange(tokens, dtype=jnp.int32)[:, None]
     )
-    bias = jnp.where(chosen & causal[None], 0.0, MASKED_SCORE).astype(jnp.bfloat16)
+    bias = jnp.where((chosen > 0.5) & causal[None], 0.0, MASKED_SCORE).astype(jnp.bfloat16)
     bias = bias.reshape(seq * tokens, window)
 
     def pooled(x):
@@ -182,50 +191,64 @@
     before = jnp.tri(tokens_here, k=-1, dtype=jnp.bfloat16)
     slot = jnp.dot(before, member.astype(jnp.bfloat16), preferred_element_type=jnp.float32)
     slot = jnp.where(member, slot.astype(jnp.int32), -1)
-    places = jnp.arange(capacity, dtype=jnp.int32)
-    at_slot = jnp.transpose(slot)[:, None, :] == places[None, :, None]
-    dispatch = at_slot.astype(jnp.bfloat16).reshape(seq_devices * capacity, tokens_here)
     route_weight = ROUTE_SCALE * route_scores / jnp.sum(route_scores, axis=1, keepdims=True)
     weight = jnp.sum(jnp.where(named, route_weight[:, :, None], 0.0), axis=1)
-    back_to = slot[:, :, None] == places[None, None, :]
     weight_parts = pieces(weight)[:2]
-    combine = jnp.where(back_to[None], weight_parts[..., None], jnp.bfloat16(0)).reshape(
-        2, tokens_here, seq_devices * capacity
-    )
-
     hidden_state = attention(queries, keys, values, branch_gates, block_choice)
-    outgoing = jnp.dot(dispatch, hidden_state, preferred_element_type=jnp.float32)
-    outgoing = outgoing.astype(jnp.bfloat16).reshape(seq_devices, capacity, features)
-    arrived = lax.all_to_all(outgoing, "seq", split_axis=0, concat_axis=0, tiled=True)
-    sources = arrived.shape[0]
-    slots = arrived.shape[1]
-    wide_rows = arrived.reshape(sources * slots, features).astype(jnp.float32)
-    squares = jnp.sum(wide_rows * wide_rows, axis=1)
-    normed = (wide_rows * norm_gain).astype(jnp.bfloat16)
-    partials = jnp.einsum("rd,dgh->rgh", normed, w_gate_up[0], preferred_element_type=jnp.float32)
-    spread = jnp.broadcast_to(squares[:, None], (squares.shape[0], lax.axis_size("exp")))
-    summed = lax.psum_scatter(
-        partials.astype(jnp.bfloat16), "exp", scatter_dimension=2, tiled=True
-    ).astype(jnp.float32)
-    square_share = lax.psum_scatter(
-        spread.astype(jnp.bfloat16), "exp", scatter_dimension=1, tiled=True
-    ).astype(jnp.float32)
-    row_scale = lax.rsqrt(square_share[:, 0] / D + EPSILON)[:, None]
-    activated = (jax.nn.silu(summed[:, 0] * row_scale) * (summed[:, 1] * row_scale)).astype(
-        jnp.bfloat16
-    )
-    down_rows = w_down[0]
-    result = jnp.dot(
-        lax.all_gather(activated, "exp", axis=1, tiled=True),
-        down_rows,
-        preferred_element_type=jnp.float32,
-    )
-    results_here = result.astype(jnp.bfloat16).reshape(sources, slots, features)
-    returned = lax.all_to_all(results_here, "seq", split_axis=0, concat_axis=0, tiled=True)
-    flattened = returned.reshape(seq_devices * capacity, features)
-    routed = jnp.dot(combine[0], flattened, preferred_element_type=jnp.float32) + jnp.dot(
-        combine[1], flattened, preferred_element_type=jnp.float32
-    )
+
+    def send(first, count):
+        places = first + jnp.arange(count, dtype=jnp.int32)
+        at_slot = jnp.transpose(slot)[:, None, :] == places[None, :, None]
+        dispatch = at_slot.astype(jnp.bfloat16).reshape(seq_devices * count, tokens_here)
+        outgoing = jnp.dot(dispatch, hidden_state, preferred_element_type=jnp.float32)
+        outgoing = outgoing.astype(jnp.bfloat16).reshape(seq_devices, count, features)
+        return lax.all_to_all(outgoing, "seq", split_axis=0, concat_axis=0, tiled=True)
+
+    def work(arrived):
+        sources, slots = arrived.shape[:2]
+        wide_rows = arrived.reshape(sources * slots, features).astype(jnp.float32)
+        squares = jnp.sum(wide_rows * wide_rows, axis=1)
+        normed = (wide_rows * norm_gain).astype(jnp.bfloat16)
+        partials = jnp.einsum(
+            "rd,dgh->rgh", normed, w_gate_up[0], preferred_element_type=jnp.float32
+        )
+        spread = jnp.broadcast_to(squares[:, None], (squares.shape[0], lax.axis_size("exp")))
+        summed = lax.psum_scatter(
+            partials.astype(jnp.bfloat16), "exp", scatter_dimension=2, tiled=True
+        ).astype(jnp.float32)
+        square_share = lax.psum_scatter(
+            spread.astype(jnp.bfloat16), "exp", scatter_dimension=1, tiled=True
+        ).astype(jnp.float32)
+        row_scale = lax.rsqrt(square_share[:, 0] / D + EPSILON)[:, None]
+        activated = (jax.nn.silu(summed[:, 0] * row_scale) * (summed[:, 1] * row_scale)).astype(
+            jnp.bfloat16
+        )
+        result = jnp.dot(
+            lax.all_gather(activated, "exp", axis=1, tiled=True),
+            w_down[0],
+            preferred_element_type=jnp.float32,
+        )
+        results_here = result.astype(jnp.bfloat16).reshape(sources, slots, features)
+        return lax.all_to_all(results_here, "seq", split_axis=0, concat_axis=0, tiled=True)
+
+    def combined(returned, first):
+        count = returned.shape[1]
+        places = first + jnp.arange(count, dtype=jnp.int32)
+        back_to = slot[:, :, None] == places[None, None, :]
+        combine = jnp.where(back_to[None], weight_parts[..., None], jnp.bfloat16(0))
+        combine = combine.reshape(2 * tokens_here, seq_devices * count)
+        both = jnp.dot(
+            combine,
+            returned.reshape(seq_devices * count, features),
+            preferred_element_type=jnp.float32,
+        )
+        return both[:tokens_here] + both[tokens_here:]
+
+    cut = -(-capacity // 32) * 16
+    firsts, counts = (0, cut), (cut, capacity - cut)
+    arrivals = [send(first, count) for first, count in zip(firsts, counts)]
+    returns = [work(arrived) for arrived in arrivals]
+    routed = combined(returns[0], firsts[0]) + combined(returns[1], firsts[1])
     return (hidden_state.astype(jnp.float32) + routed).astype(jnp.bfloat16)
 
 

time: 721 us -> 651 us (0.903)
  blocking collectives: 205 us -> 2.49 us
  waiting for transfers between devices: 330 us -> 447 us
  starting transfers between devices: 20.3 us -> 38.3 us
  local copies, waits for them, and re-layouts: 29 us -> 12.9 us
  matrix products: 70.6 us -> 83.5 us
    all_to_all x1 -> x0, blocking collectives: 203 us -> none  [local(): lax.all_to_all(outgoing, 'seq', split_axis=0, concat_axis=0, tiled=True)]
    all_to_all x1 -> x4, waiting for transfers between devices: 209 us -> 339 us  [the longest x2 172 us: send(): lax.all_to_all(outgoing, 'seq', split_axis=0, concat_axis=0, tiled=True)]
    all_to_all x1 -> x4, starting transfers between devices: 7.06 us -> 24.5 us  [the longest x2 12.4 us: work(): lax.all_to_all(results_here, 'seq', split_axis=0, concat_axis=0, tiled=True)]
    dot_general x5 -> x9, matrix products: 70.4 us -> 83.3 us  [the longest x2 42.7 us: work(): jnp.einsum('rd,dgh->rgh', normed, w_gate_up[0], preferred_element_type=jn...]
    reduce_scatter x1 -> x2, waiting for transfers between devices: 12.4 us -> 0.04 us  [work(): lax.psum_scatter(partials.astype(jnp.bfloat16), 'exp', scatter_dimension=...]
    reshape x1 -> x0, local copies, waits for them, and re-layouts: 10.8 us -> none  [attention(): chosen = jnp.broadcast_to(chosen[:, :, None, :, None], (seq, blocks_here,...]
    reduce_sum x1, other arithmetic: 12.2 us -> 3.38 us  [work(): squares = jnp.sum(wide_rows * wide_rows, axis=1)]
    convert_element_type x3 -> x7, other arithmetic: 8.3 us -> 17.1 us  [the longest x1 7.49 us: work(): normed = (wide_rows * norm_gain).astype(jnp.bfloat16)]
  transfers between devices with their start and end apart: 5 -> 10, of which waited for: 5 -> 7; matrix products, arithmetic and copies ran while one was open for 0% -> 15% of each run, Pallas kernels for 0% -> 0%
where the time goes in v2:
time: 651 us; the launch traced here: 649 us
  waiting for transfers between devices  447 us (69%)
  matrix products  83.5 us (13%)
  starting transfers between devices  38.3 us (6%)
  other arithmetic  29.2 us (4%)
  Pallas kernels  22.4 us (3%)
  between operations  13.6 us (2%)
  local copies, waits for them, and re-layouts  12.9 us (2%)
    all_to_all x2, waiting for transfers between devices, send(): lax.all_to_all(outgoing, 'seq', split_axis=0, concat_axis=0, tiled=True)  172 us
    all_to_all x2, waiting for transfers between devices, work(): lax.all_to_all(results_here, 'seq', split_axis=0, concat_axis=0, tiled=True)  167 us
    all_to_all x1, waiting for transfers between devices, attention(): got = lax.all_to_all(packed, 'seq', split_axis=0, concat_axis=0, tiled=True)  71.7 us
    dot_general x2, matrix products, work(): jnp.einsum('rd,dgh->rgh', normed, w_gate_up[0], preferred_element_type=jn...  42.7 us
    dot_general x2, matrix products, work(): jnp.dot(lax.all_gather(activated, 'exp', axis=1, tiled=True), w_down[0],...  24.2 us
    all_to_all x1, waiting for transfers between devices, attention(): lax.all_to_all(out.reshape(seq, tokens, width), 'seq', split_axis=0, conc...  23 us
    pallas_call x1, Pallas kernels, attention(): pl.pallas_call(functools.partial(attention_kernel, heads, window), grid=(...  22.4 us
  transfers between devices with their start and end apart: 10, of which 7 were waited for; matrix products, arithmetic and copies ran while one was open for 15% of the time, Pallas kernels for 0%

profile of v2, /device:TPU:28, one launch (start us, length us, event | category | flops | bytes accessed | tf_op | source)
XLA Modules:
  0.0 648.8 jit_solution(637585974511911332)
XLA Ops:
  10.3 1.8 pad_maximum_fusion
  12.1 6.9 %all-to-all-start = ((bf16[16,400,256]{2,1,0:T(8,128)(2,1)}), bf16[16,400,256]{2,1,0:T(8,128)(2,1)S(1)}, u32[]{:S(2)}, u32[]{:S(2)}) async-start(bf16[16,400,256]{2,1,0:T(8,128)(2,1)} %pad_maximum_fusion), calls=%async_computation | async-start | bytes 6553600 | tf_op jit(solution)/shard_map/all_to_all | solution.py:96
  19.9 71.7 %all-to-all-done = bf16[16,400,256]{2,1,0:T(8,128)(2,1)S(1)} async-done(((bf16[16,400,256]{2,1,0:T(8,128)(2,1)}), bf16[16,400,256]{2,1,0:T(8,128)(2,1)S(1)}, u32[]{:S(2)}, u32[]{:S(2)}) %all-to-all-start) | async-done | bytes 3276832 | tf_op jit(solution)/shard_map/all_to_all | solution.py:96
  91.7 2.0 copy.85
  94.3 2.1 slice.65
  100.0 2.0 copy.89
  103.5 22.4 %shard_map.100 = bf16[2048,256]{1,0:T(8,128)(2,1)S(1)} custom-call(bf16[2048,256]{1,0:T(8,128)(2,1)S(1)} %bitcast.133, bf16[2944,256]{1,0:T(8,128)(2,1)S(1)} %pad.30.k_ref, bf16[2944,256]{1,0:T(8,128)(2,1)S(1)} %pad.31.v_ref, bf16[32,256]{1,0:T(8,128)(2,1)S(1)} %multiply_convert_fusion.1.pk_ref, bf16[32,256]{1,0:T(8,128)(2,1)S(1)} %multiply_convert_fusion.pv_ref, ...), custom_call_target="tpu_custom_call" | custom-call | tf_op jit(solution)/shard_map/pallas_call | solution.py:151
  126.9 6.2 all-to-all-start.1
  133.6 23.0 %all-to-all-done.1 = bf16[16,128,256]{2,1,0:T(8,128)(2,1)S(1)} async-done(((bf16[16,128,256]{2,1,0:T(8,128)(2,1)}), bf16[16,128,256]{2,1,0:T(8,128)(2,1)S(1)}, u32[]{:S(2)}, u32[]{:S(2)}) %all-to-all-start.1) | async-done | bytes 1048608 | tf_op jit(solution)/shard_map/all_to_all | solution.py:167
  156.7 2.9 convolution_convert_fusion.1
  159.6 6.0 all-to-all-start.4
  165.9 4.0 convolution_convert_fusion
  169.9 74.8 %all-to-all-done.4 = bf16[16,32,3584]{2,1,0:T(8,128)(2,1)} async-done(((bf16[16,32,3584]{2,1,0:T(8,128)(2,1)}), bf16[16,32,3584]{2,1,0:T(8,128)(2,1)}, u32[]{:S(2)}, u32[]{:S(2)}) %all-to-all-start.4) | async-done | bytes 3670048 | tf_op jit(solution)/shard_map/all_to_all | solution.py:205
  244.7 6.1 all-to-all-start.2
  251.1 3.4 fusion.11
  254.5 19.0 %fusion.21 = bf16[512,2,1536]{2,0,1:T(8,128)(2,1)} fusion(bf16[512,3584,1]{1,0,2:T(8,128)(2,1)S(1)} %bitcast.153, bf16[3584,2,1536]{2,1,0:T(2,128)(2,1)} %bitcast.164), kind=kOutput, calls=%fused_computation.23 | convolution fusion | flops 11275862016 | bytes 28835840 | tf_op jit(solution)/shard_map/rd,dgh->rgh/dot_general | solution.py:212
  274.2 97.3 %all-to-all-done.2 = bf16[16,48,3584]{2,1,0:T(8,128)(2,1)} async-done(((bf16[16,48,3584]{2,1,0:T(8,128)(2,1)}), bf16[16,48,3584]{2,1,0:T(8,128)(2,1)}, u32[]{:S(2)}, u32[]{:S(2)}) %all-to-all-start.2) | async-done | bytes 5505056 | tf_op jit(solution)/shard_map/all_to_all | solution.py:205
  371.5 7.5 %fusion.4 = (bf16[16,48,3584]{2,1,0:T(8,128)(2,1)}, bf16[16,48]{1,0:T(8,128)(2,1)S(1)}) fusion(bf16[16,48,3584]{2,1,0:T(8,128)(2,1)} %all-to-all-done.2, f32[3584]{0:T(1024)S(1)} %copy-done.7), kind=kLoop, calls=%fused_computation.6 | loop fusion | flops 13761792 | bytes 11025920 | tf_op jit(solution)/shard_map/convert_element_type | solution.py:211
  379.1 2.5 all-reduce.9
  385.6 23.7 %fusion.18 = bf16[768,2,1536]{2,0,1:T(8,128)(2,1)} fusion(bf16[768,3584,1]{1,0,2:T(8,128)(2,1)} %bitcast.144, bf16[3584,2,1536]{2,1,0:T(2,128)(2,1)} %bitcast.165), kind=kOutput, calls=%fused_computation.22 | convolution fusion | flops 16913793024 | bytes 32243712 | tf_op jit(solution)/shard_map/rd,dgh->rgh/dot_general | solution.py:212
  409.3 10.4 %fusion.15 = bf16[512,3584]{1,0:T(8,128)(2,1)} fusion(bf16[512,1536]{1,0:T(8,128)(2,1)} %all-gather.5.cloned.1.call-done, bf16[1,1536,3584]{2,1,0:T(8,128)(2,1)} %param.19), kind=kOutput, calls=%fused_computation.20 | convolution fusion | flops 5638979584 | bytes 16252928 | tf_op jit(solution)/shard_map/dot_general | solution.py:226
  419.8 6.0 all-to-all-start.5
  426.4 2.0 convert_element_type.214
  428.5 1.7 fusion.26
  430.2 12.3 %all-gather.3.cloned.1.call-done = bf16[768,1536]{1,0:T(8,128)(2,1)} async-done(((bf16[768,768]{1,0:T(8,128)(2,1)}), bf16[768,1536]{1,0:T(8,128)(2,1)}) %all-gather.3.cloned.1.call-update) | async-done | bytes 2359312 | tf_op jit(solution)/shard_map/all_gather | solution.py:227
  442.5 13.7 %fusion.12 = bf16[768,3584]{1,0:T(8,128)(2,1)} fusion(bf16[768,1536]{1,0:T(8,128)(2,1)} %all-gather.3.cloned.1.call-done, bf16[1,1536,3584]{2,1,0:T(8,128)(2,1)} %param.19), kind=kOutput, calls=%fused_computation.19 | convolution fusion | flops 8458469376 | bytes 18874368 | tf_op jit(solution)/shard_map/dot_general | solution.py:226
  456.2 52.3 %all-to-all-done.5 = bf16[16,32,3584]{2,1,0:T(8,128)(2,1)} async-done(((bf16[16,32,3584]{2,1,0:T(8,128)(2,1)}), bf16[16,32,3584]{2,1,0:T(8,128)(2,1)}, u32[]{:S(2)}, u32[]{:S(2)}) %all-to-all-start.5) | async-done | bytes 3670048 | tf_op jit(solution)/shard_map/all_to_all | solution.py:232
  508.5 6.4 all-to-all-start.3
  516.2 5.0 fusion.41
  521.2 115.0 %all-to-all-done.3 = bf16[16,48,3584]{2,1,0:T(8,128)(2,1)} async-done(((bf16[16,48,3584]{2,1,0:T(8,128)(2,1)}), bf16[16,48,3584]{2,1,0:T(8,128)(2,1)}, u32[]{:S(2)}, u32[]{:S(2)}) %all-to-all-start.3) | async-done | bytes 5505056 | tf_op jit(solution)/shard_map/all_to_all | solution.py:232
  636.2 4.4 fusion.38
  640.6 1.7 fusion.30
  (103 shorter events, 19.0 us)
Async XLA Ops:
  6.5 3.2 copy-start.4
  6.5 3.3 copy-start.5
  12.1 79.6 %all-to-all-start = ((bf16[16,400,256]{2,1,0:T(8,128)(2,1)}), bf16[16,400,256]{2,1,0:T(8,128)(2,1)S(1)}, u32[]{:S(2)}, u32[]{:S(2)}) async-start(bf16[16,400,256]{2,1,0:T(8,128)(2,1)} %pad_maximum_fusion), calls=%async_computation | async-start | bytes 6553600 | tf_op jit(solution)/shard_map/all_to_all | solution.py:96
  97.8 4.2 copy-start.6
  102.0 1.2 copy-start
  102.0 1.5 copy-start.2
  103.5 29.7 %copy-start.9 = (s32[128,8]{0,1:T(8,128)S(1)}, s32[128,8]{0,1:T(8,128)}, u32[]{:S(2)}) copy-start(s32[128,8]{0,1:T(8,128)} %param.16) | copy-start | bytes 12292
  125.9 1.0 copy-start.1
  126.9 29.7 %all-to-all-start.1 = ((bf16[16,128,256]{2,1,0:T(8,128)(2,1)}), bf16[16,128,256]{2,1,0:T(8,128)(2,1)S(1)}, u32[]{:S(2)}, u32[]{:S(2)}) async-start(bf16[16,128,256]{2,1,0:T(8,128)(2,1)} %bitcast.132), calls=%async_computation.1 | async-start | bytes 2097152 | tf_op jit(solution)/shard_map/all_to_all | solution.py:167
  159.6 85.1 %all-to-all-start.4 = ((bf16[16,32,3584]{2,1,0:T(8,128)(2,1)}), bf16[16,32,3584]{2,1,0:T(8,128)(2,1)}, u32[]{:S(2)}, u32[]{:S(2)}) async-start(bf16[16,32,3584]{2,1,0:T(8,128)(2,1)} %bitcast.135), calls=%async_computation.5 | async-start | bytes 7340032 | tf_op jit(solution)/shard_map/all_to_all | solution.py:205
  244.7 6.4 copy-start.7
  244.7 126.8 %all-to-all-start.2 = ((bf16[16,48,3584]{2,1,0:T(8,128)(2,1)}), bf16[16,48,3584]{2,1,0:T(8,128)(2,1)}, u32[]{:S(2)}, u32[]{:S(2)}) async-start(bf16[16,48,3584]{2,1,0:T(8,128)(2,1)} %bitcast.134), calls=%async_computation.2 | async-start | bytes 11010048 | tf_op jit(solution)/shard_map/all_to_all | solution.py:205
  250.9 131.3 %reduce-scatter.5.cloned.1.call-start = ((), (), s32[]{:S(2)}) async-start(), calls=%async_computation.10 | async-start | bytes 4718592 | tf_op jit(solution)/shard_map/reduce_scatter | solution.py:216
  254.5 19.1 %copy-start.10 = (u32[32]{0:T(128)S(1)}, u32[32]{0:T(128)}, u32[]{:S(2)}) copy-start(u32[32]{0:T(128)} %constant.81) | copy-start | bytes 388
  273.5 135.8 %all-gather.5.cloned.1.call-start = ((), (), s32[]{:S(2)}) async-start(), calls=%async_computation.11 | async-start | bytes 2359296 | tf_op jit(solution)/shard_map/all_gather | solution.py:227
  385.3 41.1 %reduce-scatter.3.cloned.1.call-start = ((), (), s32[]{:S(2)}) async-start(), calls=%async_computation.8 | async-start | bytes 7077888 | tf_op jit(solution)/shard_map/reduce_scatter | solution.py:216
  419.8 88.7 %all-to-all-start.5 = ((bf16[16,32,3584]{2,1,0:T(8,128)(2,1)}), bf16[16,32,3584]{2,1,0:T(8,128)(2,1)}, u32[]{:S(2)}, u32[]{:S(2)}) async-start(bf16[16,32,3584]{2,1,0:T(8,128)(2,1)} %bitcast.152), calls=%async_computation.7 | async-start | bytes 7340032 | tf_op jit(solution)/shard_map/all_to_all | solution.py:232
  425.8 16.7 %all-gather.3.cloned.1.call-start = ((), (), s32[]{:S(2)}) async-start(), calls=%async_computation.9 | async-start | bytes 3538944 | tf_op jit(solution)/shard_map/all_gather | solution.py:227
  508.5 6.4 copy-start.8
  508.5 127.7 %all-to-all-start.3 = ((bf16[16,48,3584]{2,1,0:T(8,128)(2,1)}), bf16[16,48,3584]{2,1,0:T(8,128)(2,1)}, u32[]{:S(2)}, u32[]{:S(2)}) async-start(bf16[16,48,3584]{2,1,0:T(8,128)(2,1)} %bitcast.143), calls=%async_computation.4 | async-start | bytes 11010048 | tf_op jit(solution)/shard_map/all_to_all | solution.py:232
  636.2 4.4 copy-start.3
Sparse Core Ops, SparseCore 0:
  273.6 12.0 reduce-scatter.4
  385.4 10.0 all-gather.4
  409.4 12.8 reduce-scatter.2
  430.4 12.1 all-gather.2
